TPU v7x, 256 devices: a whole 4x4x8 slice. The times are simulated.
256 devices in a mesh: gx: 16 (over z, x_lo), gy: 8 (over y, x_hi), col: 2 (over core).
Axes of the slice: x: 4 (x_hi: 2, x_lo: 2; x = x_hi * 2 + x_lo), y: 4, z: 8, core: 2. Of those that a mesh axis runs over, the one named last changes fastest.
Arguments:
- source: float32 [256, 128, 512], P('gx', 'gy', 'col'), may hold values from -6 to 6
- conductance: float32 [256, 128, 512], P('gx', 'gy', 'col'), may hold values from 0.5 to 2
Outputs:
- solution: float32 [256, 128, 512], P('gx', 'gy', 'col')
- residual: float32 [256, 128, 512], P('gx', 'gy', 'col')
All inputs are finite; a program needn't handle non-finite values.
Results may differ from a plain program's by a relative error of at most 0.0003.
Values sent between devices are 32-bit elements; how exact they have to be, the bound alone decides.
A program may use at most 64 MiB of HBM per device.

v0:
```python
import functools
import math

import jax
import jax.numpy as jnp
import numpy as np
from jax import lax
from jax.experimental import pallas as pl
from jax.experimental.pallas import tpu as pltpu
from jax.sharding import PartitionSpec as P

AGG = 16
DEGREE = 3
VISITS = 3
CCYC = 4

SHIFT = 0.05
CENTER = 7.0 + SHIFT
UPPER = (8.0 + SHIFT) / CENTER
FINE_LOWER = UPPER / 4.0
COARSE_LOWER = SHIFT / CENTER
PROLONG = 0.5

NB = 16
NL = 256
W = 3
NS = NB + 2 * W
NR = 24
NW = 384
MESH = pl.DeviceIdType.MESH
HIGH = lax.Precision.HIGHEST


def cheb_poly(lower, upper):
    theta, delta = (upper + lower) / 2.0, (upper - lower) / 2.0
    sigma = theta / delta
    rho = 1.0 / sigma
    op = np.poly1d([-1.0, 8.0 + SHIFT])
    rem = np.poly1d([1.0])
    direction = rem * (1.0 / (CENTER * theta))
    total = direction
    for _ in range(DEGREE - 1):
        rem = rem - op * direction
        rho_new = 1.0 / (2.0 * sigma - rho)
        direction = (rho_new * rho) * direction + (2.0 * rho_new / delta / CENTER) * rem
        total = total + direction
        rho = rho_new
    return total


def coarse_gain(lam):
    c = cheb_poly(COARSE_LOWER, UPPER)(lam)
    err = np.zeros_like(lam)
    for _ in range(CCYC):
        err = err + c * (1.0 - (8.0 + SHIFT - lam) * err)
    return err


def sine(n):
    k = np.arange(1, n + 1)
    v = math.sqrt(2.0 / (n + 1)) * np.sin(np.pi * np.outer(k, k) / (n + 1))
    return v, 1.0 + np.cos(np.pi * k / (n + 1))


def coarse_constants(gx, gy, cz):
    vx, lx = sine(gx)
    vy, ly = sine(gy)
    vz, lz = sine(cz)
    nxh = gx // 8
    order = [(xh * 8 + xl, y) for xl in range(8) for y in range(gy) for xh in range(nxh)]
    xs = np.array([o[0] for o in order])
    ys = np.array([o[1] for o in order])
    n = len(order)
    vyx = vx[np.ix_(xs, xs)] * vy[np.ix_(ys, ys)]
    lam = (lx[xs] * ly[ys])[:, None] * lz[None, :]
    gain = np.zeros((n, 128))
    gain[:, :cz] = PROLONG * AGG ** (-1.5) * coarse_gain(lam)
    vzp = np.zeros((128, 128))
    vzp[:cz, :cz] = vz
    where = {o: i for i, o in enumerate(order)}
    table = np.zeros((gx, gy, 32, n))
    for x in range(gx):
        for y in range(gy):
            for dx in range(3):
                for dy in range(3):
                    at = where.get((x + dx - 1, y + dy - 1))
                    if at is not None:
                        table[x, y, dx * 3 + dy] = vyx[at]
                        table[x, y, 16 + dx * 3 + dy, at] = 1.0
    f32 = np.float32
    return vyx.astype(f32), vzp.astype(f32), gain.astype(f32), table.reshape(gx * gy, 32, n).astype(f32)


def dot(a, b):
    return jnp.dot(a, b, precision=HIGH, preferred_element_type=jnp.float32)


def yz_sum(v):
    v = v + pltpu.roll(v, v.shape[0] - 1, 0)
    v = v + pltpu.roll(v, 1, 0)
    v = v + pltpu.roll(v, v.shape[1] - 1, 1)
    return v + pltpu.roll(v, 1, 1)


def stencil(load, emit, first, count, group):
    before = yz_sum(load(first - 1))
    here = yz_sum(load(first))

    def body(i, carry):
        pair, here = carry
        for k in range(group):
            s = first + i * group + k
            after = yz_sum(load(s + 1))
            pair_after = here + after
            emit(s, pair + pair_after)
            pair, here = pair_after, after
        return pair, here

    lax.fori_loop(0, count // group, body, (before + here, here))


def kernel(
    size,
    src_hbm, q_hbm, vyx_hbm, vz_hbm, gain_hbm, tab_hbm,
    sol_ref, res_ref,
    src, q, vyx, vz, gain, tab,
    field, qf, one, two, total, expanded, part, sums,
    ysend, yrecv, csend, crecv, zsend, zrecv,
    g1, g2, rv, qcinv, qcsel,
    lsem, hsend, hrecv, gsend, grecv,
):
    gxn, gyn, coln = size
    nxh = gxn // 8
    gx, gy, col = lax.axis_index("gx"), lax.axis_index("gy"), lax.axis_index("col")
    other = 1 - col
    poly = cheb_poly(FINE_LOWER, UPPER).coeffs
    c2, c1, c0 = (float(c) * 8.0**-k for c, k in zip(poly, (2, 1, 0)))

    locals_ = [
        pltpu.make_async_copy(src_hbm, src, lsem.at[0]),
        pltpu.make_async_copy(q_hbm, q, lsem.at[1]),
        pltpu.make_async_copy(tab_hbm.at[gx * gyn + gy], tab, lsem.at[2]),
        pltpu.make_async_copy(vyx_hbm, vyx, lsem.at[3]),
        pltpu.make_async_copy(vz_hbm, vz, lsem.at[4]),
        pltpu.make_async_copy(gain_hbm, gain, lsem.at[5]),
    ]
    for c in locals_:
        c.start()

    row_peers = [(lax.rem(gx + d, gxn), gy, col) for d in range(1, gxn)]
    plane_peers = [
        (gx, lax.rem(gy + dy, gyn), lax.rem(col + dc, coln))
        for dy in range(gyn) for dc in range(coln) if dy or dc
    ]
    xs = (lax.rem(gx + gxn - 1, gxn), lax.rem(gx + 1, gxn))
    ys = (lax.rem(gy + gyn - 1, gyn), lax.rem(gy + 1, gyn))
    corners = [(xs[a], ys[b], col) for a in range(2) for b in range(2)]
    barrier = pltpu.get_barrier_semaphore()
    peers = row_peers + plane_peers + corners
    for p in peers:
        pl.semaphore_signal(barrier, inc=1, device_id=p, device_id_type=MESH)

    one_f = jnp.float32(1.0)
    zero_f = jnp.float32(0.0)
    x_in = (jnp.where(gx > 0, one_f, zero_f), jnp.where(gx < gxn - 1, one_f, zero_f))
    y_in = (jnp.where(gy > 0, one_f, zero_f), jnp.where(gy < gyn - 1, one_f, zero_f))
    rows = lax.broadcasted_iota(jnp.int32, (NR, NW), 0)
    lanes = lax.broadcasted_iota(jnp.int32, (NR, NW), 1)
    first_z = jnp.where(col == 0, NL, NW - 4)
    row_mask = jnp.where(rows < NB, one_f, jnp.where(rows < NB + 4, y_in[1], y_in[0]))
    lane_mask = jnp.where((lanes < NL) | ((lanes >= first_z) & (lanes < first_z + 4)), one_f, zero_f)
    mask = row_mask * lane_mask
    tile_mask = lane_mask[:, NL:]
    tile_lanes = lanes[:, :128]

    def slab_in(s):
        return jnp.where(s < W, x_in[0], jnp.where(s >= W + NB, x_in[1], one_f))

    zi = lax.broadcasted_iota(jnp.int32, (NL, 128), 0)
    li = lax.broadcasted_iota(jnp.int32, (NL, 128), 1)
    place = jnp.where((li // 16 == lax.rem(gx, 8)) & (lax.rem(li, 16) == zi // AGG), one_f, zero_f)
    ki = lax.broadcasted_iota(jnp.int32, (128, NW), 0)
    ci = lax.broadcasted_iota(jnp.int32, (128, NW), 1)
    per = NL // AGG
    coarse_of = jnp.where(
        ci < NL, col * per + ci // AGG, jnp.where(col == 0, per, per - 1)
    )
    expand = jnp.where(ki == coarse_of, one_f, zero_f)

    def block_row(acc):
        return jnp.sum(dot(acc[:8] + acc[8:], place), axis=0, keepdims=True)

    started = []

    def remote(src_ref, dst_ref, send, recv, to):
        c = pltpu.make_async_remote_copy(
            src_ref=src_ref, dst_ref=dst_ref, send_sem=send, recv_sem=recv,
            device_id=to, device_id_type=MESH,
        )
        c.start()
        return c

    def gather_rows(v):
        for p in row_peers:
            remote(g1.at[v, gx], g1.at[v, gx], gsend.at[v, 0], grecv.at[v, 0], p)

    def wait_gather(ref, sem):
        pltpu.make_async_copy(ref, ref, sem).wait()

    def gather_plane(v):
        wait_gather(g1.at[v, pl.ds(0, gxn - 1)], grecv.at[v, 0])
        slot = col * gyn + gy
        for h in range(nxh):
            tot = g1[v, h * 8]
            for k in range(1, 8):
                tot = tot + g1[v, h * 8 + k]
            for kind in range(2):
                g2[v, slot, kind * nxh + h : kind * nxh + h + 1, :] = tot[kind : kind + 1]
        for p in plane_peers:
            remote(g2.at[v, slot], g2.at[v, slot], gsend.at[v, 1], grecv.at[v, 1], p)

    def unpack_plane(v, kind):
        n = gyn * nxh
        for c in range(coln):
            for y in range(gyn):
                rv[c, y * nxh : (y + 1) * nxh, :] = g2[v, c * gyn + y, kind * nxh : (kind + 1) * nxh, :]
        low, high = rv[0], rv[1]
        lane = lax.broadcasted_iota(jnp.int32, (n, 128), 1)
        out = []
        for k in range(8):
            a = pltpu.roll(low, (128 - 16 * k) % 128, 1)
            b = pltpu.roll(high, (128 + 16 - 16 * k) % 128, 1)
            out.append(jnp.where(lane < 16, a, jnp.where(lane < 32, b, zero_f)))
        return jnp.concatenate(out, axis=0)

    def send_halo(v, buf, extra):
        copies = []
        for s in range(NB):
            t = buf[W + s, 0:NB, 0:NL]
            ysend[v, 0, W * s : W * s + W, :] = t[0:W]
            ysend[v, 1, W * s : W * s + W, :] = t[NB - W : NB]
        if extra:
            for s in range(NB):
                t = q[s]
                ysend[v, 0, 48 + s : 49 + s, :] = t[0:1]
                ysend[v, 1, 48 + s : 49 + s, :] = t[NB - 1 : NB]
        ny = 64 if extra else 48
        for b in range(2):
            copies.append(remote(
                ysend.at[v, b, pl.ds(0, ny)], yrecv.at[v, 1 - b, pl.ds(0, ny)],
                hsend.at[v, b], hrecv.at[v, 1 - b], (gx, ys[b], col)))
        for a in range(2):
            s0 = W if a == 0 else NB
            d0 = W + NB if a == 0 else 0
            copies.append(remote(
                buf.at[pl.ds(s0, W), pl.ds(0, NB), pl.ds(0, NL)],
                buf.at[pl.ds(d0, W), pl.ds(0, NB), pl.ds(0, NL)],
                hsend.at[v, 2 + a], hrecv.at[v, 2 + 1 - a], (xs[a], gy, col)))
            if extra:
                s0 = W if a == 0 else W + NB - 1
                d0 = W + NB if a == 0 else W - 1
                copies.append(remote(
                    qf.at[s0, pl.ds(0, NB), pl.ds(0, NL)],
                    qf.at[d0, pl.ds(0, NB), pl.ds(0, NL)],
                    hsend.at[v, 9 + a], hrecv.at[v, 9 + 1 - a], (xs[a], gy, col)))
        for a in range(2):
            for b in range(2):
                k = a * 2 + b
                for j in range(W):
                    s = (0 if a == 0 else NB - W) + j
                    t = buf[W + s, 0:NB, 0:NL]
                    csend[v, k, 4 * j : 4 * j + W, :] = t[0:W] if b == 0 else t[NB - W : NB]
                if extra:
                    t = q[0 if a == 0 else NB - 1]
                    csend[v, k, 3:4, :] = t[0:1] if b == 0 else t[NB - 1 : NB]
                there = (1 - a) * 2 + (1 - b)
                copies.append(remote(
                    csend.at[v, k], crecv.at[v, there],
                    hsend.at[v, 4 + k], hrecv.at[v, 4 + there], (xs[a], ys[b], col)))
        started.extend(copies)
        return copies

    def take_halo(v, buf, copies, extra):
        for c in copies:
            c.wait_recv()
        for b in range(2):
            r0 = NR - W if b == 0 else NB
            qrow = NR - 1 if b == 0 else NB
            for s in range(NB):
                buf[W + s, r0 : r0 + W, 0:NL] = yrecv[v, b, W * s : W * s + W, :] * y_in[b]
                if extra:
                    qf[W + s, qrow : qrow + 1, 0:NL] = yrecv[v, b, 48 + s : 49 + s, :] * y_in[b]
            for a in range(2):
                k = a * 2 + b
                inside = x_in[a] * y_in[b]
                d0 = 0 if a == 0 else W + NB
                for j in range(W):
                    buf[d0 + j, r0 : r0 + W, 0:NL] = crecv[v, k, 4 * j : 4 * j + W, :] * inside
                if extra:
                    d0 = W - 1 if a == 0 else W + NB
                    qf[d0, qrow : qrow + 1, 0:NL] = crecv[v, k, 3:4, :] * inside
        for a in range(2):
            d0 = 0 if a == 0 else W + NB

            @pl.when(gx == (0 if a == 0 else gxn - 1))
            def _():
                buf[pl.ds(d0, W), 0:NB, 0:NL] = jnp.zeros((W, NB, NL), jnp.float32)
                if extra:
                    qf[W - 1 if a == 0 else W + NB, 0:NB, 0:NL] = jnp.zeros((NB, NL), jnp.float32)

    inner = pl.multiple_of(other * 128, 128)

    def pack_z(buf, slabs):
        acc = jnp.zeros((NR, 128), jnp.float32)
        for s in slabs:
            t = buf[s, :, pl.ds(inner, 128)]
            acc = jnp.where(tile_lanes // 4 == s, pltpu.roll(t, 4 * s + 4 * other, 1), acc)
        return acc

    def unpack_z(acc, buf, slabs):
        for s in slabs:
            t = pltpu.roll(acc, lax.rem(128 - 4 * s - 4 * col, 128), 1)
            buf[s, :, NL:NW] = jnp.where(tile_mask > 0.5, t, zero_f)

    def send_z(v, buf, extra):
        zsend[v, 0] = pack_z(buf, range(NS))
        if extra:
            zsend[v, 1] = pack_z(qf, range(W - 1, W + NB + 1))
        n = 2 if extra else 1
        c = remote(
            zsend.at[v, pl.ds(0, n)], zrecv.at[v, pl.ds(0, n)],
            hsend.at[v, 8], hrecv.at[v, 8], (gx, gy, other))
        started.append(c)
        return c

    def take_z(v, buf, copy, extra):
        copy.wait_recv()
        unpack_z(zrecv[v, 0], buf, range(NS))
        if extra:
            unpack_z(zrecv[v, 1], qf, range(W - 1, W + NB + 1))

    for v in range(VISITS):
        for s in range(NS):
            field[v, s, NB:NR, :] = jnp.zeros((NR - NB, NW), jnp.float32)
    for s in range(W - 1, W + NB + 1):
        qf[s, NB:NR, :] = jnp.zeros((NR - NB, NW), jnp.float32)

    locals_[0].wait()
    locals_[1].wait()
    rhs_acc = jnp.zeros((NB, NL), jnp.float32)
    cond_acc = jnp.zeros((NB, NL), jnp.float32)
    for s in range(NB):
        a, b = src[s], q[s]
        rhs_acc = rhs_acc + a
        cond_acc = cond_acc + b
        field[0, W + s, 0:NB, 0:NL] = a / b
        qf[W + s, 0:NB, 0:NL] = b
    cond_row = block_row(cond_acc)

    def post(v, acc):
        g1[v, gx] = jnp.concatenate([block_row(acc), cond_row], axis=0)

    post(0, rhs_acc)
    for c in locals_[2:]:
        c.wait()
    pl.semaphore_wait(barrier, len(peers))

    for v in range(VISITS):
        extra = v == 0
        last = v == VISITS - 1
        buf = field.at[v]
        gather_rows(v)
        copies = send_halo(v, buf, extra)
        gather_plane(v)
        take_halo(v, buf, copies, extra)
        zcopy = send_z(v, buf, extra)

        wait_gather(g2.at[v, pl.ds(0, gyn * coln - 1)], grecv.at[v, 1])
        if extra:
            cond = unpack_plane(v, 1)
            inv = jnp.where(
                lax.broadcasted_iota(jnp.int32, cond.shape, 1) < per * coln, cond * (1.0 / AGG**3), one_f)
            inv = one_f / inv
            qcinv[...] = inv
            qcsel[...] = dot(tab[16:32], inv)
        t = unpack_plane(v, 0) * qcinv[...]
        t = dot(vyx[...], dot(t, vz[...])) * gain[...]
        t = dot(dot(tab[0:16], t), vz[...]) * qcsel[...]
        expanded[...] = dot(t, expand)

        take_z(v, buf, zcopy, extra)

        def emit_one(s, b):
            one[s] = mask * slab_in(s) * (c1 * buf[s] + c2 * b)

        stencil(lambda s: buf[s], emit_one, 1, NS - 2, 5)

        e = expanded[...]
        for k in range(0, 9, 3):
            part[k // 3] = jnp.where(
                rows < NB, e[k + 1 : k + 2],
                jnp.where(rows < NB + 4, e[k + 2 : k + 3], e[k : k + 1]))

        def emit_two(s, b):
            k = jnp.where(s < W, 0, jnp.where(s >= W + NB, 2, 1))
            two[s] = mask * slab_in(s) * (c0 * buf[s] + b) + qf[s] * part[k]

        stencil(lambda s: one[s], emit_two, W - 1, NB + 2, 6)

        if not last:
            sums[...] = jnp.zeros((NB, NL), jnp.float32)

        def emit_three(s, b):
            own = two[s, 0:NB, 0:NL]
            i = s - W
            rem = buf[s, 0:NB, 0:NL] - (8.0 + SHIFT) * own + 0.125 * b[0:NB, 0:NL]
            tot = own if v == 0 else total[i] + own
            if last:
                sol_ref[i] = tot / q[i]
                res_ref[i] = rem * q[i]
            else:
                total[i] = tot
                field[v + 1, s, 0:NB, 0:NL] = rem
                sums[...] += rem * q[i]

        stencil(lambda s: two[s], emit_three, W, NB, 4)

        if not last:
            post(v + 1, sums[...])

    for v in range(VISITS):
        wait_gather(g1.at[v, pl.ds(0, gxn - 1)], gsend.at[v, 0])
        wait_gather(g2.at[v, pl.ds(0, gyn * coln - 1)], gsend.at[v, 1])
    for c in started:
        c.wait_send()


def local(size, consts, source, conductance):
    gxn, gyn, coln = size
    nxh = gxn // 8
    n = gxn * gyn
    f32 = jnp.float32
    block = jax.ShapeDtypeStruct((NB, NB, NL), f32)
    vmem = pltpu.VMEM
    dma = pltpu.SemaphoreType.DMA
    return pl.pallas_call(
        functools.partial(kernel, size),
        out_shape=(block, block),
        in_specs=[pl.BlockSpec(memory_space=pl.ANY)] * 6,
        out_specs=(pl.BlockSpec(memory_space=vmem),) * 2,
        scratch_shapes=[
            vmem((NB, NB, NL), f32),
            vmem((NB, NB, NL), f32),
            vmem((n, n), f32),
            vmem((128, 128), f32),
            vmem((n, 128), f32),
            vmem((32, n), f32),
            vmem((VISITS, NS, NR, NW), f32),
            vmem((NS, NR, NW), f32),
            vmem((NS, NR, NW), f32),
            vmem((NS, NR, NW), f32),
            vmem((NB, NB, NL), f32),
            vmem((16, NW), f32),
            vmem((3, NR, NW), f32),
            vmem((NB, NL), f32),
            vmem((VISITS, 2, 64, NL), f32),
            vmem((VISITS, 2, 64, NL), f32),
            vmem((VISITS, 4, 16, NL), f32),
            vmem((VISITS, 4, 16, NL), f32),
            vmem((VISITS, 2, NR, 128), f32),
            vmem((VISITS, 2, NR, 128), f32),
            vmem((VISITS, gxn, 2, 128), f32),
            vmem((VISITS, coln * gyn, 2 * nxh, 128), f32),
            vmem((coln, gyn * nxh, 128), f32),
            vmem((n, 128), f32),
            vmem((16, 128), f32),
            dma((6,)),
            dma((VISITS, 11)),
            dma((VISITS, 11)),
            dma((VISITS, 2)),
            dma((VISITS, 2)),
        ],
        compiler_params=pltpu.CompilerParams(
            collective_id=0, has_side_effects=True, vmem_limit_bytes=48 * 1024 * 1024
        ),
    )(source, conductance, *consts)


def solution(mesh):
    size = (mesh.shape["gx"], mesh.shape["gy"], mesh.shape["col"])
    consts = coarse_constants(size[0], size[1], NL // AGG * size[2])
    spec = P("gx", "gy", "col")
    return jax.shard_map(
        lambda a, b: local(size, [jnp.asarray(c) for c in consts], a, b),
        mesh=mesh,
        in_specs=(spec, spec),
        out_specs=(spec, spec),
        check_vma=False,
    )
```

profile of v0, /device:TPU:1, one launch (start us, length us, event | category | flops | bytes accessed | tf_op | source)
XLA Modules:
  0.0 62.4 jit_solution(3533564287582423830)
XLA Ops:
  0.6 0.0 copy-start
  0.6 1.6 %copy-done = f32[128,32,128]{2,1,0:T(8,128)S(1)} copy-done((f32[128,32,128]{2,1,0:T(8,128)S(1)}, f32[128,32,128]{2,1,0:T(8,128)}, u32[]{:S(2)}) %copy-start) | copy-done | bytes 2097176
  2.2 0.0 copy-start.1
  2.2 0.9 %copy-done.1 = f32[16,16,256]{2,1,0:T(8,128)S(1)} copy-done((f32[16,16,256]{2,1,0:T(8,128)S(1)}, f32[16,16,256]{2,1,0:T(8,128)}, u32[]{:S(2)}) %copy-start.1) | copy-done | bytes 262168
  3.2 0.0 copy-start.2
  3.2 0.9 %copy-done.2 = f32[16,16,256]{2,1,0:T(8,128)S(1)} copy-done((f32[16,16,256]{2,1,0:T(8,128)S(1)}, f32[16,16,256]{2,1,0:T(8,128)}, u32[]{:S(2)}) %copy-start.2) | copy-done | bytes 262168
  4.1 0.0 copy-start.3
  4.1 0.8 %copy-done.3 = f32[128,128]{1,0:T(8,128)S(1)} copy-done((f32[128,128]{1,0:T(8,128)S(1)}, f32[128,128]{1,0:T(8,128)}, u32[]{:S(2)}) %copy-start.3) | copy-done | bytes 65560
  5.0 0.0 copy-start.4
  5.0 0.8 %copy-done.4 = f32[128,128]{1,0:T(8,128)S(1)} copy-done((f32[128,128]{1,0:T(8,128)S(1)}, f32[128,128]{1,0:T(8,128)}, u32[]{:S(2)}) %copy-start.4) | copy-done | bytes 65560
  5.8 0.0 copy-start.5
  5.8 0.8 %copy-done.5 = f32[128,128]{1,0:T(8,128)S(1)} copy-done((f32[128,128]{1,0:T(8,128)S(1)}, f32[128,128]{1,0:T(8,128)}, u32[]{:S(2)}) %copy-start.5) | copy-done | bytes 65560
  6.6 54.4 %shard_map.77 = (f32[16,16,256]{2,1,0:T(8,128)S(1)}, f32[16,16,256]{2,1,0:T(8,128)S(1)}) custom-call(f32[16,16,256]{2,1,0:T(8,128)S(1)} %copy-done.1, f32[16,16,256]{2,1,0:T(8,128)S(1)} %copy-done.2, f32[128,128]{1,0:T(8,128)S(1)} %copy-done.5, f32[128,128]{1,0:T(8,128)S(1)} %copy-done.4, f32[128,128]{1,0:T(8,128)S(1)} %copy-done.3, f32[128,32,128]{2,1,0:T(8,128)S(1)} %copy-done), custom_call_target="tpu_custom_call" | custom-call | tf_op jit(solution)/shard_map/pallas_call | solution.py:446
  61.0 0.7 %copy.10 = f32[16,16,256]{2,1,0:T(8,128)} copy(f32[16,16,256]{2,1,0:T(8,128)S(1)} %get-tuple-element.4) | data formatting | bytes 524288
  61.7 0.7 %copy.11 = f32[16,16,256]{2,1,0:T(8,128)} copy(f32[16,16,256]{2,1,0:T(8,128)S(1)} %get-tuple-element.5) | data formatting | bytes 524288
Async XLA Ops:
  0.6 1.6 %copy-start = (f32[128,32,128]{2,1,0:T(8,128)S(1)}, f32[128,32,128]{2,1,0:T(8,128)}, u32[]{:S(2)}) copy-start(f32[128,32,128]{2,1,0:T(8,128)} %constant.11.clone.tab_hbm) | copy-start | bytes 6291460
  2.2 0.9 %copy-start.1 = (f32[16,16,256]{2,1,0:T(8,128)S(1)}, f32[16,16,256]{2,1,0:T(8,128)}, u32[]{:S(2)}) copy-start(f32[16,16,256]{2,1,0:T(8,128)} %src_hbm.1) | copy-start | bytes 786436
  3.2 0.9 %copy-start.2 = (f32[16,16,256]{2,1,0:T(8,128)S(1)}, f32[16,16,256]{2,1,0:T(8,128)}, u32[]{:S(2)}) copy-start(f32[16,16,256]{2,1,0:T(8,128)} %q_hbm.1) | copy-start | bytes 786436
  4.1 0.8 %copy-start.3 = (f32[128,128]{1,0:T(8,128)S(1)}, f32[128,128]{1,0:T(8,128)}, u32[]{:S(2)}) copy-start(f32[128,128]{1,0:T(8,128)} %constant.10.clone.gain_hbm) | copy-start | bytes 196612
  5.0 0.8 %copy-start.4 = (f32[128,128]{1,0:T(8,128)S(1)}, f32[128,128]{1,0:T(8,128)}, u32[]{:S(2)}) copy-start(f32[128,128]{1,0:T(8,128)} %constant.9.clone.vz_hbm) | copy-start | bytes 196612
  5.8 0.8 %copy-start.5 = (f32[128,128]{1,0:T(8,128)S(1)}, f32[128,128]{1,0:T(8,128)}, u32[]{:S(2)}) copy-start(f32[128,128]{1,0:T(8,128)} %constant.8.clone.vyx_hbm) | copy-start | bytes 196612
where the time goes:
time: 62.7 us; the launch traced here: 62.4 us
  Pallas kernels  54.4 us (87%)
  local copies, waits for them, and re-layouts  7.41 us (12%)
  between operations  0.65 us (1%)
    pallas_call x1, Pallas kernels, local(): pl.pallas_call(functools.partial(kernel, size), out_shape=(block, block),...  54.4 us
    unnamed x14, local copies, waits for them, and re-layouts  7.41 us

commit v1 on v0

v1 whole, which is shorter than its diff:
```python
import functools
import math

import jax
import jax.numpy as jnp
import numpy as np
from jax import lax
from jax.experimental import pallas as pl
from jax.experimental.pallas import tpu as pltpu
from jax.sharding import PartitionSpec as P

AGG = 16
DEGREE = 3
VISITS = 3
CCYC = 4

SHIFT = 0.05
CENTER = 7.0 + SHIFT
UPPER = (8.0 + SHIFT) / CENTER
FINE_LOWER = UPPER / 4.0
COARSE_LOWER = SHIFT / CENTER
PROLONG = 0.5

NB = 16
NL = 256
W = 3
NS = NB + 2 * W
NR = 24
NW = 384
MESH = pl.DeviceIdType.MESH
HIGH = lax.Precision.HIGHEST


def cheb_poly(lower, upper):
    theta, delta = (upper + lower) / 2.0, (upper - lower) / 2.0
    sigma = theta / delta
    rho = 1.0 / sigma
    op = np.poly1d([-1.0, 8.0 + SHIFT])
    rem = np.poly1d([1.0])
    direction = rem * (1.0 / (CENTER * theta))
    total = direction
    for _ in range(DEGREE - 1):
        rem = rem - op * direction
        rho_new = 1.0 / (2.0 * sigma - rho)
        direction = (rho_new * rho) * direction + (2.0 * rho_new / delta / CENTER) * rem
        total = total + direction
        rho = rho_new
    return total


def coarse_gain(lam):
    c = cheb_poly(COARSE_LOWER, UPPER)(lam)
    err = np.zeros_like(lam)
    for _ in range(CCYC):
        err = err + c * (1.0 - (8.0 + SHIFT - lam) * err)
    return err


def sine(n):
    k = np.arange(1, n + 1)
    v = math.sqrt(2.0 / (n + 1)) * np.sin(np.pi * np.outer(k, k) / (n + 1))
    return v, 1.0 + np.cos(np.pi * k / (n + 1))


def coarse_constants(gx, gy, cz):
    vx, lx = sine(gx)
    vy, ly = sine(gy)
    vz, lz = sine(cz)
    order = [(x, y) for x in range(gx) for y in range(gy)]
    xs = np.array([o[0] for o in order])
    ys = np.array([o[1] for o in order])
    n = len(order)
    vyx = vx[np.ix_(xs, xs)] * vy[np.ix_(ys, ys)]
    lam = (lx[xs] * ly[ys])[:, None] * lz[None, :]
    gain = np.zeros((n, 128))
    gain[:, :cz] = PROLONG * AGG ** (-1.5) * coarse_gain(lam)
    vzp = np.zeros((128, 128))
    vzp[:cz, :cz] = vz
    where = {o: i for i, o in enumerate(order)}
    table = np.zeros((gx, gy, 32, n))
    for x in range(gx):
        for y in range(gy):
            for dx in range(3):
                for dy in range(3):
                    at = where.get((x + dx - 1, y + dy - 1))
                    if at is not None:
                        table[x, y, dx * 3 + dy] = vyx[at]
                        table[x, y, 16 + dx * 3 + dy, at] = 1.0
    f32 = np.float32
    return vyx.astype(f32), vzp.astype(f32), gain.astype(f32), table.reshape(gx * gy, 32, n).astype(f32)


def dot(a, b):
    return jnp.dot(a, b, precision=HIGH, preferred_element_type=jnp.float32)


def yz_sum(v):
    v = v + pltpu.roll(v, v.shape[0] - 1, 0)
    v = v + pltpu.roll(v, 1, 0)
    v = v + pltpu.roll(v, v.shape[1] - 1, 1)
    return v + pltpu.roll(v, 1, 1)


def stencil(load, emit, first, count, group):
    before = yz_sum(load(first - 1))
    here = yz_sum(load(first))

    def body(i, carry):
        pair, here = carry
        for k in range(group):
            s = first + i * group + k
            after = yz_sum(load(s + 1))
            pair_after = here + after
            emit(s, pair + pair_after)
            pair, here = pair_after, after
        return pair, here

    lax.fori_loop(0, count // group, body, (before + here, here))


def far_first(nz, ny):
    def ring(d, n):
        return min(d, n - d)

    every = [(dz, dy, dx) for dz in range(nz) for dy in range(ny) for dx in range(4)]
    hops = lambda d: ring(d[0], nz) + ring(d[1], ny) + ring(d[2], 4)
    return sorted((d for d in every if d != (0, 0, 0)), key=lambda d: (-hops(d), d))


def kernel(
    size,
    src_hbm, q_hbm, vyx_hbm, vz_hbm, gain_hbm, tab_hbm,
    tot_ref, rem_ref,
    src, q, vyx, vz, gain, tab,
    field, qf, one, two, expanded, part, sums,
    pair, coarse, qcinv, qcsel, vze,
    lsem, hsend, hrecv, gsend, grecv,
):
    gxn, gyn, coln = size
    gx, gy, col = lax.axis_index("gx"), lax.axis_index("gy"), lax.axis_index("col")
    other = 1 - col
    me = gx * gyn + gy
    poly = cheb_poly(FINE_LOWER, UPPER).coeffs
    c2, c1, c0 = (float(c) * 8.0**-k for c, k in zip(poly, (2, 1, 0)))

    local_copies = [
        pltpu.make_async_copy(a, b, lsem.at[k])
        for k, (a, b) in enumerate((
            (src_hbm, src), (q_hbm, q), (tab_hbm.at[me], tab),
            (vyx_hbm, vyx), (vz_hbm, vz), (gain_hbm, gain)))
    ]
    for c in local_copies:
        c.start()

    nz, ny = gxn // 2, gyn // 2
    z, y, x = gx // 2, gy // 2, lax.rem(gy, 2) * 2 + lax.rem(gx, 2)
    z_of = [lax.rem(z + d, nz) * 2 for d in range(nz)]
    y_of = [lax.rem(y + d, ny) * 2 for d in range(ny)]
    x_of = [lax.rem(x + d, 4) for d in range(4)]
    lo_of, hi_of = [lax.rem(a, 2) for a in x_of], [a // 2 for a in x_of]
    peers = [(z_of[dz] + lo_of[dx], y_of[dy] + hi_of[dx], col) for dz, dy, dx in far_first(nz, ny)]
    sibling = (gx, gy, other)

    barrier = pltpu.get_barrier_semaphore()
    for p in peers + [sibling]:
        pl.semaphore_signal(barrier, inc=1, device_id=p, device_id_type=MESH)

    xs = (lax.rem(gx + gxn - 1, gxn), lax.rem(gx + 1, gxn))
    ys = (lax.rem(gy + gyn - 1, gyn), lax.rem(gy + 1, gyn))

    one_f = jnp.float32(1.0)
    zero_f = jnp.float32(0.0)
    x_in = (jnp.where(gx > 0, one_f, zero_f), jnp.where(gx < gxn - 1, one_f, zero_f))
    y_in = (jnp.where(gy > 0, one_f, zero_f), jnp.where(gy < gyn - 1, one_f, zero_f))
    rows = lax.broadcasted_iota(jnp.int32, (NR, NW), 0)
    lanes = lax.broadcasted_iota(jnp.int32, (NR, NW), 1)
    first_z = jnp.where(col == 0, NL, NW - 4)
    row_mask = jnp.where(rows < NB, one_f, jnp.where(rows < NB + 4, y_in[1], y_in[0]))
    lane_mask = jnp.where((lanes < NL) | ((lanes >= first_z) & (lanes < first_z + 4)), one_f, zero_f)
    mask = row_mask * lane_mask

    def slab_in(s):
        return jnp.where(s < W, x_in[0], jnp.where(s >= W + NB, x_in[1], one_f))

    per = NL // AGG
    zi = lax.broadcasted_iota(jnp.int32, (NL, 128), 0) // AGG + col * per
    li = lax.broadcasted_iota(jnp.int32, (NL, 128), 1)
    place = jnp.where(li == zi, one_f, zero_f)
    ki = lax.broadcasted_iota(jnp.int32, (128, NW), 0)
    ci = lax.broadcasted_iota(jnp.int32, (128, NW), 1)
    coarse_of = jnp.where(
        ci < NL, col * per + ci // AGG, jnp.where(col == 0, per, per - 1)
    )
    valid = (ci < NL) | ((ci >= first_z) & (ci < first_z + 4))
    expand = jnp.where((ki == coarse_of) & valid, one_f, zero_f)

    def block_row(acc):
        return jnp.sum(dot(acc[:8] + acc[8:], place), axis=0, keepdims=True)

    started = []

    def remote(src_ref, dst_ref, send, recv, to):
        c = pltpu.make_async_remote_copy(
            src_ref=src_ref, dst_ref=dst_ref, send_sem=send, recv_sem=recv,
            device_id=to, device_id_type=MESH,
        )
        c.start()
        return c

    def send_pair(v, row):
        pair[v, 0:1, :] = row
        c = remote(pair.at[v, pl.ds(0, 1)], pair.at[v, pl.ds(8, 1)], hsend.at[v, 0], hrecv.at[v, 0], sibling)
        started.append(c)
        return c

    def gather(v, copy):
        copy.wait_recv()
        mine = coarse.at[v, pl.ds(me, 1)]
        mine[...] = pair[v, 0:1, :] + pair[v, 8:9, :]
        for p in peers:
            remote(mine, mine, gsend.at[v], grecv.at[v], p)

    def wait_rows(v, sem):
        ref = coarse.at[v, pl.ds(0, len(peers))]
        pltpu.make_async_copy(ref, ref, sem.at[v]).wait()

    def send_halo(v, buf, width, base):
        copies = []
        slabs = ((W, W + NB), (W + NB - width, W - width))
        lines = ((0, NB), (NB - width, NR - width))
        for a in (0, 1, None):
            for b in (0, 1, None):
                if a is None and b is None:
                    continue
                s0, s1, sn = (W, W, NB) if a is None else slabs[a] + (width,)
                r0, r1, rn = (0, 0, NB) if b is None else lines[b] + (width,)
                to = (gx if a is None else xs[a], gy if b is None else ys[b], col)
                code = lambda a, b: base + (2 if a is None else a) * 3 + (2 if b is None else b)
                there = code(None if a is None else 1 - a, None if b is None else 1 - b)
                copies.append(remote(
                    buf.at[pl.ds(s0, sn), pl.ds(r0, rn), pl.ds(0, NL)],
                    buf.at[pl.ds(s1, sn), pl.ds(r1, rn), pl.ds(0, NL)],
                    hsend.at[v, code(a, b)], hrecv.at[v, there], to))
        started.extend(copies)
        return copies

    inner = pl.multiple_of(other * 128, 128)

    def send_z(v, buf, boxes, base):
        copies = []
        for k, (s, sn, r, rn) in enumerate(boxes):
            copies.append(remote(
                buf.at[pl.ds(s, sn), pl.ds(r, rn), pl.ds(inner, 128)],
                buf.at[pl.ds(s, sn), pl.ds(r, rn), pl.ds(NL, 128)],
                hsend.at[v, base + k], hrecv.at[v, base + k], sibling))
        started.extend(copies)
        return copies

    own_box = [(W, NB, 0, NB)]

    def outer_boxes(width):
        return [(W, NB, NB, NR - NB), (W - width, width, 0, NR), (W + NB, width, 0, NR)]

    local_copies[0].wait()
    local_copies[1].wait()
    rhs_acc = jnp.zeros((NB, NL), jnp.float32)
    cond_acc = jnp.zeros((NB, NL), jnp.float32)
    for s in range(NB):
        rhs_acc = rhs_acc + src[s]
        cond_acc = cond_acc + q[s]
    row = block_row(rhs_acc) + pltpu.roll(block_row(cond_acc), 32, 1)
    for s in range(NB):
        field[0, W + s, 0:NB, 0:NL] = src[s] / q[s]
        qf[W + s, 0:NB, 0:NL] = q[s]
    for c in local_copies[2:]:
        c.wait()
    vze[...] = dot(vz[...], expand)
    pl.semaphore_wait(barrier, len(peers) + 1)

    for v in range(VISITS):
        extra = v == 0
        last = v == VISITS - 1
        buf = field.at[v]
        paired = send_pair(v, row)
        copies = send_halo(v, buf, W, 1)
        near = send_z(v, buf, own_box, 10)
        if extra:
            copies += send_halo(v, qf, 1, 14)
            near += send_z(v, qf, own_box, 23)
        gather(v, paired)
        for c in copies:
            c.wait_recv()
        near += send_z(v, buf, outer_boxes(W), 11)
        if extra:
            near += send_z(v, qf, outer_boxes(1), 24)
        wait_rows(v, grecv)
        t = coarse[v]
        if extra:
            lane = lax.broadcasted_iota(jnp.int32, t.shape, 1)
            cond = pltpu.roll(t, 96, 1) * (1.0 / AGG**3)
            inv = one_f / jnp.where(lane < per * coln, cond, one_f)
            qcinv[...] = inv
            qcsel[...] = dot(dot(tab[16:32], inv), expand)
        t = dot(vyx[...], dot(t * qcinv[...], vz[...])) * gain[...]
        expanded[...] = dot(dot(tab[0:16], t), vze[...]) * qcsel[...]
        e = expanded[...]
        for k in range(0, 9, 3):
            part[k // 3] = jnp.where(
                rows < NB, e[k + 1 : k + 2],
                jnp.where(rows < NB + 4, e[k + 2 : k + 3], e[k : k + 1]))

        for c in near:
            c.wait_recv()

        def emit_one(s, b):
            one[s] = mask * slab_in(s) * (c1 * buf[s] + c2 * b)

        stencil(lambda s: mask * slab_in(s) * buf[s], emit_one, 1, NS - 2, 5)

        def emit_two(s, b):
            k = jnp.where(s < W, 0, jnp.where(s >= W + NB, 2, 1))
            two[s] = mask * slab_in(s) * (c0 * buf[s] + b) + qf[s] * part[k]

        stencil(lambda s: one[s], emit_two, W - 1, NB + 2, 6)

        if not last:
            sums[...] = jnp.zeros((NB, NL), jnp.float32)

        def emit_three(s, b):
            own = two[s, 0:NB, 0:NL]
            i = s - W
            rem = buf[s, 0:NB, 0:NL] - (8.0 + SHIFT) * own + 0.125 * b[0:NB, 0:NL]
            tot_ref[i] = own if v == 0 else tot_ref[i] + own
            if last:
                rem_ref[i] = rem
            else:
                field[v + 1, s, 0:NB, 0:NL] = rem
                sums[...] += rem * q[i]

        stencil(lambda s: two[s], emit_three, W, NB, 4)

        if not last:
            row = block_row(sums[...])

    for v in range(VISITS):
        wait_rows(v, gsend)
    for c in started:
        c.wait_send()


def local(size, consts, source, conductance):
    gxn, gyn, coln = size
    n = gxn * gyn
    f32 = jnp.float32
    block = jax.ShapeDtypeStruct((NB, NB, NL), f32)
    vmem = pltpu.VMEM
    dma = pltpu.SemaphoreType.DMA
    total, remainder = pl.pallas_call(
        functools.partial(kernel, size),
        out_shape=(block, block),
        in_specs=[pl.BlockSpec(memory_space=pl.ANY)] * 6,
        out_specs=(pl.BlockSpec(memory_space=vmem),) * 2,
        scratch_shapes=[
            vmem((NB, NB, NL), f32),
            vmem((NB, NB, NL), f32),
            vmem((n, n), f32),
            vmem((128, 128), f32),
            vmem((n, 128), f32),
            vmem((32, n), f32),
            vmem((VISITS, NS, NR, NW), f32),
            vmem((NS, NR, NW), f32),
            vmem((NS, NR, NW), f32),
            vmem((NS, NR, NW), f32),
            vmem((16, NW), f32),
            vmem((3, NR, NW), f32),
            vmem((NB, NL), f32),
            vmem((VISITS, 16, 128), f32),
            vmem((VISITS, n, 128), f32),
            vmem((n, 128), f32),
            vmem((16, NW), f32),
            vmem((128, NW), f32),
            dma((6,)),
            dma((VISITS, 27)),
            dma((VISITS, 27)),
            dma((VISITS,)),
            dma((VISITS,)),
        ],
        compiler_params=pltpu.CompilerParams(
            collective_id=0, has_side_effects=True, vmem_limit_bytes=60 * 1024 * 1024
        ),
    )(source, conductance, *consts)
    return total / conductance, remainder * conductance


def solution(mesh):
    size = (mesh.shape["gx"], mesh.shape["gy"], mesh.shape["col"])
    consts = coarse_constants(size[0], size[1], NL // AGG * size[2])
    spec = P("gx", "gy", "col")
    return jax.shard_map(
        lambda a, b: local(size, [jnp.asarray(c) for c in consts], a, b),
        mesh=mesh,
        in_specs=(spec, spec),
        out_specs=(spec, spec),
        check_vma=False,
    )
```

time: 62.7 us -> 56.4 us (0.90)
  local copies, waits for them, and re-layouts: 7.41 us -> 0.01 us
  other arithmetic: 0 us -> 1.88 us
    unnamed x14 -> x2, local copies, waits for them, and re-layouts: 7.41 us -> 0.01 us
    mul x0 -> x1, other arithmetic: none -> 1.88 us  [local(): return (total / conductance, remainder * conductance)]
where the time goes in v1:
time: 56.4 us; the launch traced here: 56.3 us
  Pallas kernels  53.8 us (95%)
  other arithmetic  1.88 us (3%)
  between operations  0.65 us (1%)
    pallas_call x1, Pallas kernels, local(): pl.pallas_call(functools.partial(kernel, size), out_shape=(block, block),...  53.8 us
    mul x1, other arithmetic, local(): return (total / conductance, remainder * conductance)  1.88 us

profile of v1, /device:TPU:1, one launch (start us, length us, event | category | flops | bytes accessed | tf_op | source)
XLA Modules:
  0.0 56.3 jit_solution(8370402149480528469)
XLA Ops:
  0.6 0.0 copy-start
  0.6 53.8 %shard_map.77 = (f32[16,16,256]{2,1,0:T(8,128)}, f32[16,16,256]{2,1,0:T(8,128)}) custom-call(f32[16,16,256]{2,1,0:T(8,128)} %src_hbm.1, f32[16,16,256]{2,1,0:T(8,128)} %q_hbm.1, f32[128,128]{1,0:T(8,128)} %constant.8.clone.vyx_hbm, f32[128,128]{1,0:T(8,128)} %constant.9.clone.vz_hbm, f32[128,128]{1,0:T(8,128)} %constant.10.clone.gain_hbm, ...), custom_call_target="tpu_custom_call" | custom-call | tf_op jit(solution)/shard_map/pallas_call | solution.py:358
  54.5 0.0 copy-done
  54.5 1.9 %fusion = (f32[16,16,256]{2,1,0:T(8,128)}, f32[16,16,256]{2,1,0:T(8,128)}) fusion(f32[16,16,256]{2,1,0:T(8,128)} %get-tuple-element.5, f32[16,16,256]{2,1,0:T(8,128)S(1)} %copy-done, f32[16,16,256]{2,1,0:T(8,128)} %get-tuple-element.4), kind=kLoop, calls=%fused_computation | loop fusion | flops 131072 | bytes 1310720 | tf_op jit(solution)/shard_map/mul | solution.py:392
Async XLA Ops:
  0.6 53.8 %copy-start = (f32[16,16,256]{2,1,0:T(8,128)S(1)}, f32[16,16,256]{2,1,0:T(8,128)}, u32[]{:S(2)}) copy-start(f32[16,16,256]{2,1,0:T(8,128)} %q_hbm.1) | copy-start | bytes 786436

commit v2 on v1

--- a/solution.py
+++ b/solution.py
@@ -28,6 +28,8 @@
 NR = 24
 NW = 384
 MESH = pl.DeviceIdType.MESH
+G1, G2, G3 = 10, 9, 8
+HALO_ORDER = ((None, 0), (None, 1), (0, 0), (0, 1), (1, 0), (1, 1), (0, None), (1, None))
 HIGH = lax.Precision.HIGHEST
 
 
@@ -102,29 +104,31 @@
 
 
 def stencil(load, emit, first, count, group):
-    before = yz_sum(load(first - 1))
-    here = yz_sum(load(first))
+    here = load(first)
 
     def body(i, carry):
         pair, here = carry
         for k in range(group):
             s = first + i * group + k
-            after = yz_sum(load(s + 1))
+            after = load(s + 1)
             pair_after = here + after
-            emit(s, pair + pair_after)
+            emit(s, yz_sum(pair + pair_after))
             pair, here = pair_after, after
         return pair, here
 
-    lax.fori_loop(0, count // group, body, (before + here, here))
-
-
-def far_first(nz, ny):
+    carry = (load(first - 1) + here, here)
+    if group == count:
+        body(0, carry)
+    else:
+        lax.fori_loop(0, count // group, body, carry)
+
+
+def far_first(ny):
     def ring(d, n):
         return min(d, n - d)
 
-    every = [(dz, dy, dx) for dz in range(nz) for dy in range(ny) for dx in range(4)]
-    hops = lambda d: ring(d[0], nz) + ring(d[1], ny) + ring(d[2], 4)
-    return sorted((d for d in every if d != (0, 0, 0)), key=lambda d: (-hops(d), d))
+    every = [(dy, dx) for dy in range(ny) for dx in range(4)]
+    return sorted(every, key=lambda d: (-ring(d[0], ny) - ring(d[1], 4), d))
 
 
 def kernel(
@@ -154,16 +158,34 @@
 
     nz, ny = gxn // 2, gyn // 2
     z, y, x = gx // 2, gy // 2, lax.rem(gy, 2) * 2 + lax.rem(gx, 2)
-    z_of = [lax.rem(z + d, nz) * 2 for d in range(nz)]
     y_of = [lax.rem(y + d, ny) * 2 for d in range(ny)]
     x_of = [lax.rem(x + d, 4) for d in range(4)]
     lo_of, hi_of = [lax.rem(a, 2) for a in x_of], [a // 2 for a in x_of]
-    peers = [(z_of[dz] + lo_of[dx], y_of[dy] + hi_of[dx], col) for dz, dy, dx in far_first(nz, ny)]
+    plane = far_first(ny)
+    n_peers = nz * ny * 4 - 1
+
+    def each_peer(act):
+        def planes(k, carry):
+            dz = nz // 2 + jnp.where(lax.rem(k, 2) == 0, k // 2, -((k + 1) // 2))
+            z_of = lax.rem(z + dz, nz) * 2
+            for dy, dx in plane:
+                act((z_of + lo_of[dx], y_of[dy] + hi_of[dx], col))
+            return carry
+
+        lax.fori_loop(0, nz - 1, planes, 0)
+        for dy, dx in plane:
+            if dy or dx:
+                act((z * 2 + lo_of[dx], y_of[dy] + hi_of[dx], col))
+
     sibling = (gx, gy, other)
 
     barrier = pltpu.get_barrier_semaphore()
-    for p in peers + [sibling]:
+
+    def greet(p):
         pl.semaphore_signal(barrier, inc=1, device_id=p, device_id_type=MESH)
+
+    each_peer(greet)
+    greet(sibling)
 
     xs = (lax.rem(gx + gxn - 1, gxn), lax.rem(gx + 1, gxn))
     ys = (lax.rem(gy + gyn - 1, gyn), lax.rem(gy + 1, gyn))
@@ -197,63 +219,61 @@
     def block_row(acc):
         return jnp.sum(dot(acc[:8] + acc[8:], place), axis=0, keepdims=True)
 
-    started = []
-
     def remote(src_ref, dst_ref, send, recv, to):
-        c = pltpu.make_async_remote_copy(
+        return pltpu.make_async_remote_copy(
             src_ref=src_ref, dst_ref=dst_ref, send_sem=send, recv_sem=recv,
             device_id=to, device_id_type=MESH,
         )
-        c.start()
-        return c
-
-    def send_pair(v, row):
-        pair[v, 0:1, :] = row
-        c = remote(pair.at[v, pl.ds(0, 1)], pair.at[v, pl.ds(8, 1)], hsend.at[v, 0], hrecv.at[v, 0], sibling)
-        started.append(c)
-        return c
-
-    def gather(v, copy):
-        copy.wait_recv()
+
+    def start(copies):
+        for c in copies:
+            c.start()
+
+    def received(copies):
+        for c in copies:
+            c.wait_recv()
+
+    def sent(copies):
+        for c in copies:
+            c.wait_send()
+
+    def pair_copy(v):
+        return remote(pair.at[v, pl.ds(0, 1)], pair.at[v, pl.ds(8, 1)], hsend.at[v, 0], hrecv.at[v, 0], sibling)
+
+    def gather(v):
         mine = coarse.at[v, pl.ds(me, 1)]
         mine[...] = pair[v, 0:1, :] + pair[v, 8:9, :]
-        for p in peers:
-            remote(mine, mine, gsend.at[v], grecv.at[v], p)
+        each_peer(lambda p: remote(mine, mine, gsend.at[v], grecv.at[v], p).start())
 
     def wait_rows(v, sem):
-        ref = coarse.at[v, pl.ds(0, len(peers))]
+        ref = coarse.at[v, pl.ds(0, n_peers)]
         pltpu.make_async_copy(ref, ref, sem.at[v]).wait()
 
-    def send_halo(v, buf, width, base):
+    def halo_copies(v, buf, width, base):
         copies = []
         slabs = ((W, W + NB), (W + NB - width, W - width))
         lines = ((0, NB), (NB - width, NR - width))
-        for a in (0, 1, None):
-            for b in (0, 1, None):
-                if a is None and b is None:
-                    continue
-                s0, s1, sn = (W, W, NB) if a is None else slabs[a] + (width,)
-                r0, r1, rn = (0, 0, NB) if b is None else lines[b] + (width,)
-                to = (gx if a is None else xs[a], gy if b is None else ys[b], col)
-                code = lambda a, b: base + (2 if a is None else a) * 3 + (2 if b is None else b)
-                there = code(None if a is None else 1 - a, None if b is None else 1 - b)
-                copies.append(remote(
-                    buf.at[pl.ds(s0, sn), pl.ds(r0, rn), pl.ds(0, NL)],
-                    buf.at[pl.ds(s1, sn), pl.ds(r1, rn), pl.ds(0, NL)],
-                    hsend.at[v, code(a, b)], hrecv.at[v, there], to))
-        started.extend(copies)
+        for a, b in HALO_ORDER:
+            s0, s1, sn = (W, W, NB) if a is None else slabs[a] + (width,)
+            r0, r1, rn = (0, 0, NB) if b is None else lines[b] + (width,)
+            to = (gx if a is None else xs[a], gy if b is None else ys[b], col)
+            code = lambda a, b: base + (2 if a is None else a) * 3 + (2 if b is None else b)
+            there = code(None if a is None else 1 - a, None if b is None else 1 - b)
+            copies.append(remote(
+                buf.at[pl.ds(s0, sn), pl.ds(r0, rn), pl.ds(0, NL)],
+                buf.at[pl.ds(s1, sn), pl.ds(r1, rn), pl.ds(0, NL)],
+                hsend.at[v, code(a, b)], hrecv.at[v, there], to))
         return copies
 
     inner = pl.multiple_of(other * 128, 128)
 
-    def send_z(v, buf, boxes, base):
+    def z_copies(v, buf, boxes, base):
         copies = []
         for k, (s, sn, r, rn) in enumerate(boxes):
             copies.append(remote(
                 buf.at[pl.ds(s, sn), pl.ds(r, rn), pl.ds(inner, 128)],
                 buf.at[pl.ds(s, sn), pl.ds(r, rn), pl.ds(NL, 128)],
                 hsend.at[v, base + k], hrecv.at[v, base + k], sibling))
-        started.extend(copies)
         return copies
 
     own_box = [(W, NB, 0, NB)]
@@ -268,40 +288,58 @@
     for s in range(NB):
         rhs_acc = rhs_acc + src[s]
         cond_acc = cond_acc + q[s]
-    row = block_row(rhs_acc) + pltpu.roll(block_row(cond_acc), 32, 1)
+    pair[0, 0:1, :] = block_row(rhs_acc) + pltpu.roll(block_row(cond_acc), 32, 1)
     for s in range(NB):
         field[0, W + s, 0:NB, 0:NL] = src[s] / q[s]
         qf[W + s, 0:NB, 0:NL] = q[s]
+        tot_ref[s] = jnp.zeros((NB, NL), jnp.float32)
     for c in local_copies[2:]:
         c.wait()
     vze[...] = dot(vz[...], expand)
-    pl.semaphore_wait(barrier, len(peers) + 1)
-
-    for v in range(VISITS):
-        extra = v == 0
-        last = v == VISITS - 1
+    pl.semaphore_wait(barrier, n_peers + 1)
+
+    def visit(v, carry):
+        first = v == 0
         buf = field.at[v]
-        paired = send_pair(v, row)
-        copies = send_halo(v, buf, W, 1)
-        near = send_z(v, buf, own_box, 10)
-        if extra:
-            copies += send_halo(v, qf, 1, 14)
-            near += send_z(v, qf, own_box, 23)
-        gather(v, paired)
-        for c in copies:
-            c.wait_recv()
-        near += send_z(v, buf, outer_boxes(W), 11)
-        if extra:
-            near += send_z(v, qf, outer_boxes(1), 24)
+        paired = pair_copy(v)
+        halo = halo_copies(v, buf, W, 1)
+        near = z_copies(v, buf, own_box, 10)
+        far = z_copies(v, buf, outer_boxes(W), 11)
+
+        def q_halo():
+            return halo_copies(v, qf, 1, 14)
+
+        def q_near():
+            return z_copies(v, qf, own_box, 23)
+
+        def q_far():
+            return z_copies(v, qf, outer_boxes(1), 24)
+
+        start([paired] + halo + near)
+
+        @pl.when(first)
+        def _():
+            start(q_halo() + q_near())
+
+        received([paired])
+        gather(v)
+        received(halo)
+        start(far)
+
+        @pl.when(first)
+        def _():
+            received(q_halo())
+            start(q_far())
+
         wait_rows(v, grecv)
-        t = coarse[v]
-        if extra:
-            lane = lax.broadcasted_iota(jnp.int32, t.shape, 1)
-            cond = pltpu.roll(t, 96, 1) * (1.0 / AGG**3)
+        @pl.when(first)
+        def _():
+            lane = lax.broadcasted_iota(jnp.int32, (gxn * gyn, 128), 1)
+            cond = pltpu.roll(coarse[v], 96, 1) * (1.0 / AGG**3)
             inv = one_f / jnp.where(lane < per * coln, cond, one_f)
             qcinv[...] = inv
             qcsel[...] = dot(dot(tab[16:32], inv), expand)
-        t = dot(vyx[...], dot(t * qcinv[...], vz[...])) * gain[...]
+        t = dot(vyx[...], dot(coarse[v] * qcinv[...], vz[...])) * gain[...]
         expanded[...] = dot(dot(tab[0:16], t), vze[...]) * qcsel[...]
         e = expanded[...]
         for k in range(0, 9, 3):
@@ -309,55 +347,61 @@
                 rows < NB, e[k + 1 : k + 2],
                 jnp.where(rows < NB + 4, e[k + 2 : k + 3], e[k : k + 1]))
 
-        for c in near:
-            c.wait_recv()
+        received(near + far)
 
         def emit_one(s, b):
             one[s] = mask * slab_in(s) * (c1 * buf[s] + c2 * b)
 
-        stencil(lambda s: mask * slab_in(s) * buf[s], emit_one, 1, NS - 2, 5)
+        stencil(lambda s: mask * slab_in(s) * buf[s], emit_one, 1, NS - 2, G1)
 
         def emit_two(s, b):
             k = jnp.where(s < W, 0, jnp.where(s >= W + NB, 2, 1))
             two[s] = mask * slab_in(s) * (c0 * buf[s] + b) + qf[s] * part[k]
 
-        stencil(lambda s: one[s], emit_two, W - 1, NB + 2, 6)
-
-        if not last:
-            sums[...] = jnp.zeros((NB, NL), jnp.float32)
+        @pl.when(first)
+        def _():
+            received(q_near() + q_far())
+
+        stencil(lambda s: one[s], emit_two, W - 1, NB + 2, G2)
+
+        sums[...] = jnp.zeros((NB, NL), jnp.float32)
 
         def emit_three(s, b):
             own = two[s, 0:NB, 0:NL]
             i = s - W
             rem = buf[s, 0:NB, 0:NL] - (8.0 + SHIFT) * own + 0.125 * b[0:NB, 0:NL]
-            tot_ref[i] = own if v == 0 else tot_ref[i] + own
-            if last:
-                rem_ref[i] = rem
-            else:
-                field[v + 1, s, 0:NB, 0:NL] = rem
-                sums[...] += rem * q[i]
-
-        stencil(lambda s: two[s], emit_three, W, NB, 4)
-
-        if not last:
-            row = block_row(sums[...])
-
-    for v in range(VISITS):
+            tot_ref[i] += own
+            rem_ref[i] = rem
+            field[v + 1, s, 0:NB, 0:NL] = rem
+            sums[...] += rem * q[i]
+
+        stencil(lambda s: two[s], emit_three, W, NB, G3)
+
+        @pl.when(v < VISITS - 1)
+        def _():
+            pair[v + 1, 0:1, :] = block_row(sums[...])
+
+        sent([paired] + halo + near + far)
         wait_rows(v, gsend)
-    for c in started:
-        c.wait_send()
+
+        @pl.when(first)
+        def _():
+            sent(q_halo() + q_near() + q_far())
+
+        return carry
+
+    lax.fori_loop(0, VISITS, visit, 0)
 
 
 def local(size, consts, source, conductance):
     gxn, gyn, coln = size
     n = gxn * gyn
     f32 = jnp.float32
-    block = jax.ShapeDtypeStruct((NB, NB, NL), f32)
     vmem = pltpu.VMEM
     dma = pltpu.SemaphoreType.DMA
     total, remainder = pl.pallas_call(
         functools.partial(kernel, size),
-        out_shape=(block, block),
+        out_shape=(vmem((NB, NB, NL), f32),) * 2,
         in_specs=[pl.BlockSpec(memory_space=pl.ANY)] * 6,
         out_specs=(pl.BlockSpec(memory_space=vmem),) * 2,
         scratch_shapes=[
@@ -367,7 +411,7 @@
             vmem((128, 128), f32),
             vmem((n, 128), f32),
             vmem((32, n), f32),
-            vmem((VISITS, NS, NR, NW), f32),
+            vmem((VISITS + 1, NS, NR, NW), f32),
             vmem((NS, NR, NW), f32),
             vmem((NS, NR, NW), f32),
             vmem((NS, NR, NW), f32),

time: 56.4 us -> 51.1 us (0.906)
  Pallas kernels: 53.8 us -> 49.5 us
  other arithmetic: 1.88 us -> 0.85 us
    pallas_call x1, Pallas kernels: 53.8 us -> 49.5 us  [local(): pl.pallas_call(functools.partial(kernel, size), out_shape=(vmem((NB, NB,...]
    mul x1, other arithmetic: 1.88 us -> 0.85 us  [local(): return (total / conductance, remainder * conductance)]
where the time goes in v2:
time: 51.1 us; the launch traced here: 51 us
  Pallas kernels  49.5 us (97%)
  other arithmetic  0.85 us (2%)
  between operations  0.65 us (1%)
    pallas_call x1, Pallas kernels, local(): pl.pallas_call(functools.partial(kernel, size), out_shape=(vmem((NB, NB,...  49.5 us

profile of v2, /device:TPU:1, one launch (start us, length us, event | category | flops | bytes accessed | tf_op | source)
XLA Modules:
  0.0 51.0 jit_solution(6349029044823492317)
XLA Ops:
  0.6 0.0 copy-start
  0.6 49.5 %shard_map.77 = (f32[16,16,256]{2,1,0:T(8,128)S(1)}, f32[16,16,256]{2,1,0:T(8,128)S(1)}) custom-call(f32[16,16,256]{2,1,0:T(8,128)} %src_hbm.1, f32[16,16,256]{2,1,0:T(8,128)} %q_hbm.1, f32[128,128]{1,0:T(8,128)} %constant.8.clone.vyx_hbm, f32[128,128]{1,0:T(8,128)} %constant.9.clone.vz_hbm, f32[128,128]{1,0:T(8,128)} %constant.10.clone.gain_hbm, ...), custom_call_target="tpu_custom_call" | custom-call | tf_op jit(solution)/shard_map/pallas_call | solution.py:402
  50.2 0.0 copy-done
  50.2 0.8 %fusion = (f32[16,16,256]{2,1,0:T(8,128)}, f32[16,16,256]{2,1,0:T(8,128)}) fusion(f32[16,16,256]{2,1,0:T(8,128)S(1)} %get-tuple-element.5, f32[16,16,256]{2,1,0:T(8,128)S(1)} %copy-done, f32[16,16,256]{2,1,0:T(8,128)S(1)} %get-tuple-element.4), kind=kLoop, calls=%fused_computation | loop fusion | flops 131072 | bytes 1310720 | tf_op jit(solution)/shard_map/mul | solution.py:436
Async XLA Ops:
  0.6 49.5 %copy-start = (f32[16,16,256]{2,1,0:T(8,128)S(1)}, f32[16,16,256]{2,1,0:T(8,128)}, u32[]{:S(2)}) copy-start(f32[16,16,256]{2,1,0:T(8,128)} %q_hbm.1) | copy-start | bytes 786436

commit v3 on v2

--- a/solution.py
+++ b/solution.py
@@ -28,7 +28,7 @@
 NR = 24
 NW = 384
 MESH = pl.DeviceIdType.MESH
-G1, G2, G3 = 10, 9, 8
+G1, G2, G3 = 20, 18, 16
 HALO_ORDER = ((None, 0), (None, 1), (0, 0), (0, 1), (1, 0), (1, 1), (0, None), (1, None))
 HIGH = lax.Precision.HIGHEST
 
@@ -96,24 +96,38 @@
     return jnp.dot(a, b, precision=HIGH, preferred_element_type=jnp.float32)
 
 
-def yz_sum(v):
+def y_sum(v):
     v = v + pltpu.roll(v, v.shape[0] - 1, 0)
-    v = v + pltpu.roll(v, 1, 0)
-    v = v + pltpu.roll(v, v.shape[1] - 1, 1)
-    return v + pltpu.roll(v, 1, 1)
-
-
-def stencil(load, emit, first, count, group):
+    return v + pltpu.roll(v, 1, 0)
+
+
+def z_matrix():
+    i = lax.broadcasted_iota(jnp.int32, (NW, NW), 0)
+    j = lax.broadcasted_iota(jnp.int32, (NW, NW), 1)
+    d = jnp.abs(i - j)
+    return jnp.where(d == 0, 2.0, jnp.where((d == 1) | (d == NW - 1), 1.0, 0.0)).astype(jnp.bfloat16)
+
+
+def z_sum(v, tz):
+    high = v.astype(jnp.bfloat16)
+    low = (v - high.astype(jnp.float32)).astype(jnp.bfloat16)
+    return jnp.dot(jnp.concatenate([high, low], axis=1), tz, preferred_element_type=jnp.float32)
+
+
+def stencil(load, emit, tz, first, count, group, rows=NR):
     here = load(first)
 
     def body(i, carry):
         pair, here = carry
+        out = []
         for k in range(group):
-            s = first + i * group + k
-            after = load(s + 1)
+            after = load(first + i * group + k + 1)
             pair_after = here + after
-            emit(s, yz_sum(pair + pair_after))
+            out.append(y_sum(pair + pair_after)[:rows])
             pair, here = pair_after, after
+        out = z_sum(jnp.concatenate(out, axis=0), tz)
+        for k in range(group):
+            emit(first + i * group + k, out[k * rows : (k + 1) * rows])
         return pair, here
 
     carry = (load(first - 1) + here, here)
@@ -137,7 +151,7 @@
     tot_ref, rem_ref,
     src, q, vyx, vz, gain, tab,
     field, qf, one, two, expanded, part, sums,
-    pair, coarse, qcinv, qcsel, vze,
+    pair, coarse, qcinv, qcsel, vze, tz,
     lsem, hsend, hrecv, gsend, grecv,
 ):
     gxn, gyn, coln = size
@@ -296,6 +310,9 @@
     for c in local_copies[2:]:
         c.wait()
     vze[...] = dot(vz[...], expand)
+    t = z_matrix()
+    tz[0:NW, :] = t
+    tz[NW:, :] = t
     pl.semaphore_wait(barrier, n_peers + 1)
 
     def visit(v, carry):
@@ -315,7 +332,7 @@
         def q_far():
             return z_copies(v, qf, outer_boxes(1), 24)
 
-        start([paired] + halo + near)
+        start([paired] + halo[:2])
 
         @pl.when(first)
         def _():
@@ -323,6 +340,7 @@
 
         received([paired])
         gather(v)
+        start(halo[2:] + near)
         received(halo)
         start(far)
 
@@ -352,7 +370,7 @@
         def emit_one(s, b):
             one[s] = mask * slab_in(s) * (c1 * buf[s] + c2 * b)
 
-        stencil(lambda s: mask * slab_in(s) * buf[s], emit_one, 1, NS - 2, G1)
+        stencil(lambda s: mask * slab_in(s) * buf[s], emit_one, tz[...], 1, NS - 2, G1)
 
         def emit_two(s, b):
             k = jnp.where(s < W, 0, jnp.where(s >= W + NB, 2, 1))
@@ -362,20 +380,20 @@
         def _():
             received(q_near() + q_far())
 
-        stencil(lambda s: one[s], emit_two, W - 1, NB + 2, G2)
+        stencil(lambda s: one[s], emit_two, tz[...], W - 1, NB + 2, G2)
 
         sums[...] = jnp.zeros((NB, NL), jnp.float32)
 
         def emit_three(s, b):
             own = two[s, 0:NB, 0:NL]
             i = s - W
-            rem = buf[s, 0:NB, 0:NL] - (8.0 + SHIFT) * own + 0.125 * b[0:NB, 0:NL]
+            rem = buf[s, 0:NB, 0:NL] - (8.0 + SHIFT) * own + 0.125 * b
             tot_ref[i] += own
             rem_ref[i] = rem
             field[v + 1, s, 0:NB, 0:NL] = rem
             sums[...] += rem * q[i]
 
-        stencil(lambda s: two[s], emit_three, W, NB, G3)
+        stencil(lambda s: two[s], emit_three, tz[:, 0:NL], W, NB, G3, NB)
 
         @pl.when(v < VISITS - 1)
         def _():
@@ -423,6 +441,7 @@
             vmem((n, 128), f32),
             vmem((16, NW), f32),
             vmem((128, NW), f32),
+            vmem((2 * NW, NW), jnp.bfloat16),
             dma((6,)),
             dma((VISITS, 27)),
             dma((VISITS, 27)),

time: 51.1 us -> 49.1 us (0.961)
  Pallas kernels: 49.5 us -> 47.5 us
    pallas_call x1, Pallas kernels: 49.5 us -> 47.5 us  [local(): pl.pallas_call(functools.partial(kernel, size), out_shape=(vmem((NB, NB,...]
where the time goes in v3:
time: 49.1 us; the launch traced here: 49 us
  Pallas kernels  47.5 us (97%)
  other arithmetic  0.85 us (2%)
  between operations  0.65 us (1%)
    pallas_call x1, Pallas kernels, local(): pl.pallas_call(functools.partial(kernel, size), out_shape=(vmem((NB, NB,...  47.5 us

profile of v3, /device:TPU:1, one launch (start us, length us, event | category | flops | bytes accessed | tf_op | source)
XLA Modules:
  0.0 49.0 jit_solution(18219655960720052710)
XLA Ops:
  0.6 0.0 copy-start
  0.6 47.5 %shard_map.77 = (f32[16,16,256]{2,1,0:T(8,128)S(1)}, f32[16,16,256]{2,1,0:T(8,128)S(1)}) custom-call(f32[16,16,256]{2,1,0:T(8,128)} %src_hbm.1, f32[16,16,256]{2,1,0:T(8,128)} %q_hbm.1, f32[128,128]{1,0:T(8,128)} %constant.8.clone.vyx_hbm, f32[128,128]{1,0:T(8,128)} %constant.9.clone.vz_hbm, f32[128,128]{1,0:T(8,128)} %constant.10.clone.gain_hbm, ...), custom_call_target="tpu_custom_call" | custom-call | tf_op jit(solution)/shard_map/pallas_call | solution.py:420
  48.1 0.0 copy-done
  48.1 0.8 %fusion = (f32[16,16,256]{2,1,0:T(8,128)}, f32[16,16,256]{2,1,0:T(8,128)}) fusion(f32[16,16,256]{2,1,0:T(8,128)S(1)} %get-tuple-element.5, f32[16,16,256]{2,1,0:T(8,128)S(1)} %copy-done, f32[16,16,256]{2,1,0:T(8,128)S(1)} %get-tuple-element.4), kind=kLoop, calls=%fused_computation | loop fusion | flops 131072 | bytes 1310720 | tf_op jit(solution)/shard_map/mul | solution.py:455
Async XLA Ops:
  0.6 47.5 %copy-start = (f32[16,16,256]{2,1,0:T(8,128)S(1)}, f32[16,16,256]{2,1,0:T(8,128)}, u32[]{:S(2)}) copy-start(f32[16,16,256]{2,1,0:T(8,128)} %q_hbm.1) | copy-start | bytes 786436

commit v4 on v3

--- a/solution.py
+++ b/solution.py
@@ -96,6 +96,35 @@
     return jnp.dot(a, b, precision=HIGH, preferred_element_type=jnp.float32)
 
 
+def halves(v):
+    high = v.astype(jnp.bfloat16)
+    return high, (v - high.astype(jnp.float32)).astype(jnp.bfloat16)
+
+
+def right(v):
+    high, low = halves(v)
+    return jnp.concatenate([high, high, low], axis=0)
+
+
+def left(v):
+    high, low = halves(v)
+    return jnp.concatenate([high, high, low], axis=1)
+
+
+def data_left(v):
+    high, low = halves(v)
+    return jnp.concatenate([high, low, high], axis=1)
+
+
+def data_right(v):
+    high, low = halves(v)
+    return jnp.concatenate([high, low, high], axis=0)
+
+
+def dot3(a, b):
+    return jnp.dot(a, b, preferred_element_type=jnp.float32)
+
+
 def y_sum(v):
     v = v + pltpu.roll(v, v.shape[0] - 1, 0)
     return v + pltpu.roll(v, 1, 0)
@@ -151,7 +180,7 @@
     tot_ref, rem_ref,
     src, q, vyx, vz, gain, tab,
     field, qf, one, two, expanded, part, sums,
-    pair, coarse, qcinv, qcsel, vze, tz,
+    pair, coarse, qcinv, qcsel, vze3, vz3, vyx3, tab3, place2, tz,
     lsem, hsend, hrecv, gsend, grecv,
 ):
     gxn, gyn, coln = size
@@ -231,7 +260,8 @@
     expand = jnp.where((ki == coarse_of) & valid, one_f, zero_f)
 
     def block_row(acc):
-        return jnp.sum(dot(acc[:8] + acc[8:], place), axis=0, keepdims=True)
+        parts = jnp.concatenate(halves(acc[:8] + acc[8:]), axis=1)
+        return jnp.sum(dot3(parts, place2[...]), axis=0, keepdims=True)
 
     def remote(src_ref, dst_ref, send, recv, to):
         return pltpu.make_async_remote_copy(
@@ -295,6 +325,9 @@
     def outer_boxes(width):
         return [(W, NB, NB, NR - NB), (W - width, width, 0, NR), (W + NB, width, 0, NR)]
 
+    half = place.astype(jnp.bfloat16)
+    place2[0:NL, :] = half
+    place2[NL:, :] = half
     local_copies[0].wait()
     local_copies[1].wait()
     rhs_acc = jnp.zeros((NB, NL), jnp.float32)
@@ -309,7 +342,10 @@
         tot_ref[s] = jnp.zeros((NB, NL), jnp.float32)
     for c in local_copies[2:]:
         c.wait()
-    vze[...] = dot(vz[...], expand)
+    vze3[...] = right(dot(vz[...], expand))
+    vz3[...] = right(vz[...])
+    vyx3[...] = left(vyx[...])
+    tab3[...] = left(tab[0:16])
     t = z_matrix()
     tz[0:NW, :] = t
     tz[NW:, :] = t
@@ -357,8 +393,10 @@
             inv = one_f / jnp.where(lane < per * coln, cond, one_f)
             qcinv[...] = inv
             qcsel[...] = dot(dot(tab[16:32], inv), expand)
-        t = dot(vyx[...], dot(coarse[v] * qcinv[...], vz[...])) * gain[...]
-        expanded[...] = dot(dot(tab[0:16], t), vze[...]) * qcsel[...]
+        t = dot3(data_left(coarse[v] * qcinv[...]), vz3[...])
+        t = dot3(vyx3[...], data_right(t)) * gain[...]
+        t = dot3(tab3[...], data_right(t))
+        expanded[...] = dot3(data_left(t), vze3[...]) * qcsel[...]
         e = expanded[...]
         for k in range(0, 9, 3):
             part[k // 3] = jnp.where(
@@ -440,7 +478,11 @@
             vmem((VISITS, n, 128), f32),
             vmem((n, 128), f32),
             vmem((16, NW), f32),
-            vmem((128, NW), f32),
+            vmem((384, NW), jnp.bfloat16),
+            vmem((384, 128), jnp.bfloat16),
+            vmem((n, 3 * n), jnp.bfloat16),
+            vmem((16, 3 * n), jnp.bfloat16),
+            vmem((2 * NL, 128), jnp.bfloat16),
             vmem((2 * NW, NW), jnp.bfloat16),
             dma((6,)),
             dma((VISITS, 27)),

time: 49.1 us -> 48.8 us (level)
  no operation moved by 1% of the time
where the time goes in v4:
time: 48.8 us; the launch traced here: 48.7 us
  Pallas kernels  47.2 us (97%)
  other arithmetic  0.85 us (2%)
  between operations  0.65 us (1%)
    pallas_call x1, Pallas kernels, local(): pl.pallas_call(functools.partial(kernel, size), out_shape=(vmem((NB, NB,...  47.2 us

profile of v4, /device:TPU:1, one launch (start us, length us, event | category | flops | bytes accessed | tf_op | source)
XLA Modules:
  0.0 48.7 jit_solution(8874863360603515186)
XLA Ops:
  0.6 0.0 copy-start
  0.6 47.2 %shard_map.77 = (f32[16,16,256]{2,1,0:T(8,128)S(1)}, f32[16,16,256]{2,1,0:T(8,128)S(1)}) custom-call(f32[16,16,256]{2,1,0:T(8,128)} %src_hbm.1, f32[16,16,256]{2,1,0:T(8,128)} %q_hbm.1, f32[128,128]{1,0:T(8,128)} %constant.8.clone.vyx_hbm, f32[128,128]{1,0:T(8,128)} %constant.9.clone.vz_hbm, f32[128,128]{1,0:T(8,128)} %constant.10.clone.gain_hbm, ...), custom_call_target="tpu_custom_call" | custom-call | tf_op jit(solution)/shard_map/pallas_call | solution.py:458
  47.8 0.0 copy-done
  47.8 0.8 %fusion = (f32[16,16,256]{2,1,0:T(8,128)}, f32[16,16,256]{2,1,0:T(8,128)}) fusion(f32[16,16,256]{2,1,0:T(8,128)S(1)} %get-tuple-element.5, f32[16,16,256]{2,1,0:T(8,128)S(1)} %copy-done, f32[16,16,256]{2,1,0:T(8,128)S(1)} %get-tuple-element.4), kind=kLoop, calls=%fused_computation | loop fusion | flops 131072 | bytes 1310720 | tf_op jit(solution)/shard_map/mul | solution.py:497
Async XLA Ops:
  0.6 47.2 %copy-start = (f32[16,16,256]{2,1,0:T(8,128)S(1)}, f32[16,16,256]{2,1,0:T(8,128)}, u32[]{:S(2)}) copy-start(f32[16,16,256]{2,1,0:T(8,128)} %q_hbm.1) | copy-start | bytes 786436

commit v5 on v4

--- a/solution.py
+++ b/solution.py
@@ -392,7 +392,11 @@
             cond = pltpu.roll(coarse[v], 96, 1) * (1.0 / AGG**3)
             inv = one_f / jnp.where(lane < per * coln, cond, one_f)
             qcinv[...] = inv
-            qcsel[...] = dot(dot(tab[16:32], inv), expand)
+            pick = tab[16:32].astype(jnp.bfloat16)
+            near_inv = dot3(jnp.concatenate([pick, pick], axis=1), jnp.concatenate(halves(inv), axis=0))
+            spread = expand.astype(jnp.bfloat16)
+            qcsel[...] = dot3(
+                jnp.concatenate(halves(near_inv), axis=1), jnp.concatenate([spread, spread], axis=0))
         t = dot3(data_left(coarse[v] * qcinv[...]), vz3[...])
         t = dot3(vyx3[...], data_right(t)) * gain[...]
         t = dot3(tab3[...], data_right(t))

time: 48.8 us -> 48.7 us (level)
  no operation moved by 1% of the time
where the time goes in v5:
time: 48.7 us; the launch traced here: 48.6 us
  Pallas kernels  47.1 us (97%)
  other arithmetic  0.85 us (2%)
  between operations  0.65 us (1%)
    pallas_call x1, Pallas kernels, local(): pl.pallas_call(functools.partial(kernel, size), out_shape=(vmem((NB, NB,...  47.1 us

profile of v5, /device:TPU:1, one launch (start us, length us, event | category | flops | bytes accessed | tf_op | source)
XLA Modules:
  0.0 48.6 jit_solution(8245032173827468622)
XLA Ops:
  0.6 0.0 copy-start
  0.6 47.1 %shard_map.77 = (f32[16,16,256]{2,1,0:T(8,128)S(1)}, f32[16,16,256]{2,1,0:T(8,128)S(1)}) custom-call(f32[16,16,256]{2,1,0:T(8,128)} %src_hbm.1, f32[16,16,256]{2,1,0:T(8,128)} %q_hbm.1, f32[128,128]{1,0:T(8,128)} %constant.8.clone.vyx_hbm, f32[128,128]{1,0:T(8,128)} %constant.9.clone.vz_hbm, f32[128,128]{1,0:T(8,128)} %constant.10.clone.gain_hbm, ...), custom_call_target="tpu_custom_call" | custom-call | tf_op jit(solution)/shard_map/pallas_call | solution.py:462
  47.7 0.0 copy-done
  47.8 0.8 %fusion = (f32[16,16,256]{2,1,0:T(8,128)}, f32[16,16,256]{2,1,0:T(8,128)}) fusion(f32[16,16,256]{2,1,0:T(8,128)S(1)} %get-tuple-element.5, f32[16,16,256]{2,1,0:T(8,128)S(1)} %copy-done, f32[16,16,256]{2,1,0:T(8,128)S(1)} %get-tuple-element.4), kind=kLoop, calls=%fused_computation | loop fusion | flops 131072 | bytes 1310720 | tf_op jit(solution)/shard_map/mul | solution.py:501
Async XLA Ops:
  0.6 47.1 %copy-start = (f32[16,16,256]{2,1,0:T(8,128)S(1)}, f32[16,16,256]{2,1,0:T(8,128)}, u32[]{:S(2)}) copy-start(f32[16,16,256]{2,1,0:T(8,128)} %q_hbm.1) | copy-start | bytes 786436
